TPU v7x, 512 devices: a whole 4x8x8 slice. The times are simulated.
512 devices in a mesh: lon: 32 (over z_lo, y, core), ch: 16 (over x, z_hi).
Axes of the slice: x: 4, y: 8, z: 8 (z_hi: 4, z_lo: 2; z = z_hi * 2 + z_lo), core: 2. Of those that a mesh axis runs over, the one named last changes fastest.
Arguments:
- grid_state: bfloat16 [128, 512, 1024], P(None, 'lon', 'ch'), may hold values from -40 to 40
- first_gain: bfloat16 [1024], P('ch'), may hold values from 0.099609375 to 1.8984375
- spectral_first: bfloat16 [2, 1024, 64], P(None, 'ch'), may hold values from -0.5 to 0.5
- spectral_second: bfloat16 [2, 1024, 64], P(None, 'ch'), may hold values from -0.5 to 0.5
- second_gain: bfloat16 [1024], P('ch'), may hold values from 0.099609375 to 1.8984375
- up_weight: bfloat16 [1024, 4096], P(None, 'ch'), may hold values from -0.1875 to 0.1875
- down_weight: bfloat16 [4096, 1024], P('ch'), may hold values from -0.125 to 0.125
Outputs:
- block_out: bfloat16 [128, 512, 1024], P(None, 'lon', 'ch')
All inputs are finite; a program needn't handle non-finite values.
Results may differ from a plain program's by a relative error of at most 0.015.
Values may be sent and summed in bfloat16 or wider, within the bound.
No kernel may reach another device: no remote copies, remote signals or barrier semaphores. Data moves between devices by JAX's collectives and lax.ppermute only.
A program may use at most 64 MiB of HBM per device.

v0:
```python
import math
import jax
import jax.numpy as jnp
from jax import lax
from jax.sharding import PartitionSpec as P

H = 128
W = 512
C = 1024
KW = 256
EPSILON = 1e-05
THRESHOLD = 0.1
HIGHEST = lax.Precision.HIGHEST


def dft_tables(length, harmonics):
    sample_idx = jnp.arange(length, dtype=jnp.int32)[:, None]
    harmonic_idx = jnp.arange(harmonics, dtype=jnp.int32)[None, :]
    phase = (sample_idx * harmonic_idx % length).astype(jnp.float32) * (2.0 * math.pi / length)
    factor = 1.0 / math.sqrt(length)
    return (jnp.cos(phase) * factor, jnp.sin(phase) * factor)


def normalize(values, total, square, gain, width):
    centre = total[..., None] / width
    spread = square[..., None] / width - centre * centre
    return ((values - centre) * lax.rsqrt(spread + EPSILON) * gain).astype(jnp.bfloat16)


def soft_shrink(values):
    return values - jnp.clip(values, -THRESHOLD, THRESHOLD)


def lat_apply(values, table):
    return jnp.einsum("kch,hq->kcq", values, table, precision=HIGHEST)


def complex_mix(real_part, imag_part, weight):
    mode_len, chan_len, lat_len = real_part.shape
    block_width = weight.shape[-1]
    blocks = chan_len // block_width
    w_real = weight[0].reshape(blocks, block_width, block_width)
    w_imag = weight[1].reshape(blocks, block_width, block_width)
    real_blocks = real_part.reshape(mode_len, blocks, block_width, lat_len)
    imag_blocks = imag_part.reshape(mode_len, blocks, block_width, lat_len)

    def product(left, right):
        return jnp.einsum("knbq,nbd->kndq", left, right, preferred_element_type=jnp.float32)

    new_real = product(real_blocks, w_real) - product(imag_blocks, w_imag)
    new_imag = product(real_blocks, w_imag) + product(imag_blocks, w_real)
    return (
        new_real.reshape(mode_len, chan_len, lat_len),
        new_imag.reshape(mode_len, chan_len, lat_len),
    )


def per_device(
    grid_state, first_gain, spectral_first, spectral_second, second_gain, up_weight, down_weight
):
    lat_count, col_count, chan_count = grid_state.shape
    values = grid_state.astype(jnp.float32)
    total_one, square_one = lax.psum(
        (jnp.sum(values, axis=2), jnp.sum(values * values, axis=2)), "ch"
    )
    normed_first = normalize(values, total_one, square_one, first_gain, C)
    columns = lax.all_to_all(normed_first, "lon", split_axis=2, concat_axis=1, tiled=True)
    lon_cos, lon_sin = dft_tables(W, KW)
    lat_cos, lat_sin = dft_tables(H, H)
    column_data = columns.astype(jnp.float32)
    fwd_real = jnp.einsum("hwc,wk->kch", column_data, lon_cos, precision=HIGHEST)
    fwd_imag = -jnp.einsum("hwc,wk->kch", column_data, lon_sin, precision=HIGHEST)
    spec_real = lat_apply(fwd_real, lat_cos) + lat_apply(fwd_imag, lat_sin)
    spec_imag = lat_apply(fwd_imag, lat_cos) - lat_apply(fwd_real, lat_sin)
    modes = lax.all_to_all(
        jnp.stack([spec_real, spec_imag]).astype(jnp.bfloat16),
        "lon",
        split_axis=1,
        concat_axis=2,
        tiled=True,
    )
    mid_real, mid_imag = complex_mix(modes[0], modes[1], spectral_first)
    mid_real = jax.nn.relu(mid_real).astype(jnp.bfloat16)
    mid_imag = jax.nn.relu(mid_imag).astype(jnp.bfloat16)
    out_real, out_imag = complex_mix(mid_real, mid_imag, spectral_second)
    out_real = soft_shrink(out_real)
    out_imag = soft_shrink(out_imag)
    inv_real = lat_apply(out_real, lat_cos) - lat_apply(out_imag, lat_sin)
    inv_imag = lat_apply(out_imag, lat_cos) + lat_apply(out_real, lat_sin)
    returned = lax.all_to_all(
        jnp.stack([inv_real, inv_imag]).astype(jnp.bfloat16),
        "lon",
        split_axis=2,
        concat_axis=1,
        tiled=True,
    ).astype(jnp.float32)
    back_real = returned[0]
    back_imag = returned[1]
    harmonic_weight = jnp.where(jnp.arange(KW, dtype=jnp.int32) == 0, 1.0, 2.0).astype(jnp.float32)
    inv_cos = lon_cos * harmonic_weight[None, :]
    inv_sin = lon_sin * harmonic_weight[None, :]
    grid_cols = jnp.einsum("kch,wk->hwc", back_real, inv_cos, precision=HIGHEST)
    grid_cols = grid_cols - jnp.einsum("kch,wk->hwc", back_imag, inv_sin, precision=HIGHEST)
    filtered = lax.all_to_all(
        grid_cols.astype(jnp.bfloat16), "lon", split_axis=1, concat_axis=2, tiled=True
    )
    mixed = (values + normed_first.astype(jnp.float32) + filtered.astype(jnp.float32)).astype(
        jnp.bfloat16
    )
    mixed_wide = mixed.astype(jnp.float32)
    token_count = lat_count * col_count
    everything, whole_gain = (
        lax.all_gather(mixed, "ch", axis=2, tiled=True),
        lax.all_gather(second_gain, "ch", axis=0, tiled=True),
    )
    spread_all = everything.astype(jnp.float32)
    normed_second = normalize(
        spread_all,
        jnp.sum(spread_all, axis=2),
        jnp.sum(spread_all * spread_all, axis=2),
        whole_gain,
        C,
    )
    upward = jnp.dot(
        normed_second.reshape(token_count, C), up_weight, preferred_element_type=jnp.float32
    )
    hidden = jax.nn.gelu(upward).astype(jnp.bfloat16)
    summed = lax.psum_scatter(
        jnp.einsum("tj,jc->ct", hidden, down_weight, preferred_element_type=jnp.float32).astype(
            jnp.bfloat16
        ),
        "ch",
        scatter_dimension=0,
        tiled=True,
    ).astype(jnp.float32)
    branch = summed.T.reshape(lat_count, col_count, chan_count)
    return (mixed_wide + branch).astype(jnp.bfloat16)


def solution(mesh):
    return jax.shard_map(
        per_device,
        mesh=mesh,
        in_specs=(
            P(None, "lon", "ch"),
            P("ch"),
            P(None, "ch", None),
            P(None, "ch", None),
            P("ch"),
            P(None, "ch"),
            P("ch", None),
        ),
        out_specs=P(None, "lon", "ch"),
        check_vma=False,
    )
```

profile of v0, /device:TPU:1, one launch (start us, length us, event | category | flops | bytes accessed | tf_op | source)
XLA Modules:
  0.0 401.5 jit_solution(9092841457983095221)
XLA Ops:
  6.5 1.2 convert_reduce_fusion.1
  7.7 0.7 convert_element_type.105
  8.4 74.7 %all-reduce.1 = (f32[128,16]{0,1:T(8,128)S(1)}, f32[128,16]{0,1:T(8,128)S(1)}) all-reduce(f32[128,16]{0,1:T(8,128)S(1)} %get-tuple-element.8, f32[128,16]{0,1:T(8,128)S(1)} %get-tuple-element.7), channel_id=1, replica_groups=mesh['lon'=32,'ch'=16] {'ch'}, use_global_device_ids=true, to_apply=%region_3.0 | all-reduce | flops 4096 | bytes 32768 | tf_op jit(solution)/shard_map/psum | solution.py:63
  83.0 1.1 fusion.41
  84.2 34.5 %all_to_all.57 = bf16[128,16,64]{0,1,2:T(8,128)(2,1)S(1)} all-to-all(bf16[128,16,64]{0,1,2:T(8,128)(2,1)S(1)} %fusion.41), channel_id=1, replica_groups=mesh['lon'=32,'ch'=16] {'lon'}, dimensions={2} | all-to-all | bytes 524288 | tf_op jit(solution)/shard_map/all_to_all | solution.py:67
  118.8 2.7 convolution_bitcast_fusion
  121.4 2.7 fusion.17
  124.1 0.6 fusion.80
  124.8 0.6 fusion.78
  125.4 0.6 fusion.30
  126.0 0.6 fusion.29
  126.7 0.3 copy.123
  127.0 16.2 %all_to_all.58 = bf16[2,256,2,128]{3,2,0,1:T(2,128)(2,1)S(1)} all-to-all(bf16[2,256,2,128]{3,2,0,1:T(2,128)(2,1)S(1)} %copy.123), channel_id=1, replica_groups=mesh['lon'=32,'ch'=16] {'lon'}, dimensions={1} | all-to-all | bytes 524288 | tf_op jit(solution)/shard_map/all_to_all | solution.py:75
  143.1 0.2 copy.162
  143.4 0.2 fusion.184
  143.6 0.2 fusion.107
  143.8 0.2 fusion.111
  144.0 0.2 fusion.26
  144.4 0.2 fusion.101
  144.6 0.2 fusion.25
  144.9 0.2 clamp_subtract_fusion.1
  145.1 0.6 fusion.76
  145.7 0.2 clamp_subtract_fusion
  145.9 0.6 fusion.74
  146.5 0.6 fusion.28
  147.2 0.6 fusion.27
  147.8 0.9 copy.129
  148.7 5.0 %all-to-all-start.2 = ((bf16[2,8,64,128]{3,1,0,2:T(8,128)(2,1)}), bf16[2,8,64,128]{3,1,0,2:T(8,128)(2,1)S(1)}, u32[]{:S(2)}, u32[]{:S(2)}) async-start(bf16[2,8,64,128]{3,1,0,2:T(8,128)(2,1)} %copy.129), calls=%async_computation.2 | async-start | bytes 524288 | tf_op jit(solution)/shard_map/all_to_all | solution.py:90
  153.7 0.2 all-gather.2.cloned.1.call-start
  154.0 11.8 %all-to-all-done.2 = bf16[2,8,64,128]{3,1,0,2:T(8,128)(2,1)S(1)} async-done(((bf16[2,8,64,128]{3,1,0,2:T(8,128)(2,1)}), bf16[2,8,64,128]{3,1,0,2:T(8,128)(2,1)S(1)}, u32[]{:S(2)}, u32[]{:S(2)}) %all-to-all-start.2) | async-done | bytes 262176 | tf_op jit(solution)/shard_map/all_to_all | solution.py:90
  165.8 2.3 fusion.48
  168.1 2.5 fusion.18
  170.7 0.3 copy.131
  170.9 16.2 %all_to_all.59 = bf16[128,512,2]{0,2,1:T(2,128)(2,1)S(1)} all-to-all(bf16[128,512,2]{0,2,1:T(2,128)(2,1)S(1)} %copy.131), channel_id=1, replica_groups=mesh['lon'=32,'ch'=16] {'lon'}, dimensions={1} | all-to-all | bytes 524288 | tf_op jit(solution)/shard_map/all_to_all | solution.py:104
  187.3 0.9 fusion.44
  188.3 1.3 dynamic-slice
  190.2 0.2 dynamic-update-slice
  190.4 32.4 %all-reduce = bf16[1024]{0:T(1024)(128)(2,1)S(1)} all-reduce(bf16[1024]{0:T(1024)(128)(2,1)S(1)} %dynamic-update-slice), channel_id=1, replica_groups=mesh['lon'=32,'ch'=16] {'ch'}, use_global_device_ids=true, to_apply=%add | all-reduce | flops 1024 | bytes 4096
  222.8 37.9 %all-gather.2.cloned.1.call-done = bf16[128,16,1024]{0,1,2:T(8,128)(2,1)} async-done(((bf16[128,16,64]{0,1,2:T(8,128)(2,1)}), bf16[128,16,1024]{0,1,2:T(8,128)(2,1)}) %all-gather.2.cloned.1.call-update) | async-done | bytes 4194320 | tf_op jit(solution)/shard_map/all_gather | solution.py:113
  260.7 7.4 %copy.134 = bf16[128,16,1024]{2,1,0:T(8,128)(2,1)} copy(bf16[128,16,1024]{0,1,2:T(8,128)(2,1)} %all-gather.2.cloned.1.call-done) | data formatting | bytes 8388608 | tf_op jit(solution)/shard_map/all_gather | solution.py:113
  268.2 3.6 convert_reduce_fusion
  272.1 4.4 %fusion.2 = bf16[128,16,1024]{2,1,0:T(8,128)(2,1)} fusion(bf16[128,16,1024]{2,1,0:T(8,128)(2,1)} %copy.134, f32[1024]{0:T(1024)S(1)} %convert_element_type.123, f32[128,16]{1,0:T(8,128)S(1)} %copy.138, f32[128,16]{1,0:T(8,128)S(1)} %copy.136), kind=kLoop, calls=%fused_computation.5 | loop fusion | flops 10485760 | bytes 8409088 | tf_op jit(solution)/shard_map/convert_element_type | solution.py:27
  276.5 8.5 %convert_bitcast_fusion = bf16[1024,2048]{0,1:T(8,128)(2,1)} fusion(bf16[256,1024]{1,0:T(8,128)(2,1)S(1)} %copy-done, bf16[2048,1024]{1,0:T(8,128)(2,1)} %bitcast.168, bf16[1024,256]{1,0:T(8,128)(2,1)S(1)} %copy-done.5), kind=kOutput, calls=%fused_computation.7 | convolution fusion | flops 2154299392 | bytes 9437184 | tf_op jit(solution)/shard_map/tj,jc->ct/dot_general | solution.py:129
  284.9 6.5 %copy.147 = bf16[1024,2048]{1,0:T(8,128)(2,1)} copy(bf16[1024,2048]{0,1:T(8,128)(2,1)} %convert_bitcast_fusion) | data formatting | bytes 8388608
  291.5 100.5 %reduce-scatter.4.cloned.1.call-done = bf16[64,2048]{1,0:T(8,128)(2,1)} async-done(((bf16[1024,2048]{1,0:T(8,128)(2,1)}), bf16[64,2048]{1,0:T(8,128)(2,1)}) %reduce-scatter.4.cloned.1.call-update) | async-done | bytes 262160
  392.0 1.2 copy.148
  393.3 0.6 copy.139
  393.9 0.8 copy.140
  (36 shorter events, 1.1 us)
Async XLA Ops:
  6.5 269.9 %copy-start = (bf16[256,1024]{1,0:T(8,128)(2,1)S(1)}, bf16[256,1024]{1,0:T(8,128)(2,1)}, u32[]{:S(2)}) copy-start(bf16[256,1024]{1,0:T(8,128)(2,1)} %param.13) | copy-start | bytes 1572868
  121.4 22.1 %copy-start.3 = (bf16[2,64,64]{2,1,0:T(8,128)(2,1)S(1)}, bf16[2,64,64]{2,1,0:T(8,128)(2,1)}, u32[]{:S(2)}) copy-start(bf16[2,64,64]{2,1,0:T(8,128)(2,1)} %param.9) | copy-start | bytes 49156
  121.4 22.8 %copy-start.4 = (bf16[2,64,64]{2,1,0:T(8,128)(2,1)S(1)}, bf16[2,64,64]{2,1,0:T(8,128)(2,1)}, u32[]{:S(2)}) copy-start(bf16[2,64,64]{2,1,0:T(8,128)(2,1)} %param.10) | copy-start | bytes 49156
  148.7 17.1 %all-to-all-start.2 = ((bf16[2,8,64,128]{3,1,0,2:T(8,128)(2,1)}), bf16[2,8,64,128]{3,1,0,2:T(8,128)(2,1)S(1)}, u32[]{:S(2)}, u32[]{:S(2)}) async-start(bf16[2,8,64,128]{3,1,0,2:T(8,128)(2,1)} %copy.129), calls=%async_computation.2 | async-start | bytes 524288 | tf_op jit(solution)/shard_map/all_to_all | solution.py:90
  153.7 107.0 %all-gather.2.cloned.1.call-start = ((), (), s32[]{:S(2)}) async-start(), calls=%async_computation.5 | async-start | bytes 4456448 | tf_op jit(solution)/shard_map/all_gather | solution.py:113
  165.8 21.4 %copy-start.1 = (bf16[128,16,64]{0,2,1:T(8,128)(2,1)S(1)}, bf16[128,16,64]{0,2,1:T(8,128)(2,1)}, u32[]{:S(2)}) copy-start(bf16[128,16,64]{0,2,1:T(8,128)(2,1)} %param.7) | copy-start | bytes 786436
  168.1 22.1 %copy-start.6 = (bf16[64]{0:T(256)(128)(2,1)S(1)}, bf16[64]{0:T(256)(128)(2,1)}, u32[]{:S(2)}) copy-start(bf16[64]{0:T(256)(128)(2,1)} %param.11) | copy-start | bytes 388
  188.2 203.8 %reduce-scatter.4.cloned.1.call-start = ((), (), s32[]{:S(2)}) async-start(), calls=%async_computation.6 | async-start | bytes 4456448
  272.1 4.4 %copy-start.5 = (bf16[1024,256]{1,0:T(8,128)(2,1)S(1)}, bf16[1024,256]{1,0:T(8,128)(2,1)}, u32[]{:S(2)}) copy-start(bf16[1024,256]{1,0:T(8,128)(2,1)} %param.12) | copy-start | bytes 1572868
  291.5 102.4 %copy-start.2 = (bf16[128,16,64]{0,1,2:T(8,128)(2,1)S(1)}, bf16[128,16,64]{0,1,2:T(8,128)(2,1)}, u32[]{:S(2)}) copy-start(bf16[128,16,64]{0,1,2:T(8,128)(2,1)} %fusion.44) | copy-start | bytes 786436
Sparse Core Ops, SparseCore 0:
  188.3 72.3 all-gather.1
  291.6 100.3 reduce-scatter.3
where the time goes:
time: 402 us
  blocking collectives  174 us (43%)
  waiting for transfers between devices  150 us (37%)
  matrix products  25.2 us (6%)
  local copies, waits for them, and re-layouts  20.4 us (5%)
  between operations  14.4 us (4%)
  other arithmetic  12.1 us (3%)
  starting transfers between devices  5.27 us (1%)
    unnamed x3, waiting for transfers between devices  101 us
    psum x1, blocking collectives, per_device(): lax.psum((jnp.sum(values, axis=2), jnp.sum(values * values, axis=2)), 'ch')  74.7 us
    all_gather x1, waiting for transfers between devices, per_device(): lax.all_gather(mixed, 'ch', axis=2, tiled=True)  37.9 us
    all_to_all x1, blocking collectives, per_device(): lax.all_to_all(normed_first, 'lon', split_axis=2, concat_axis=1, tiled=True)  34.5 us
    unnamed x1, blocking collectives  32.4 us
    all_to_all x1, blocking collectives, per_device(): lax.all_to_all(grid_cols.astype(jnp.bfloat16), 'lon', split_axis=1, conca...  16.2 us
    all_to_all x1, blocking collectives, per_device(): lax.all_to_all(jnp.stack([spec_real, spec_imag]).astype(jnp.bfloat16), 'l...  16.2 us
    all_to_all x1, waiting for transfers between devices, per_device(): lax.all_to_all(jnp.stack([inv_real, inv_imag]).astype(jnp.bfloat16), 'lon...  11.8 us
  transfers between devices with their start and end apart: 3, of which 3 were waited for; matrix products, arithmetic and copies ran while one was open for 0% of the time, Pallas kernels for 0%

commit v1 on v0

--- a/solution.py
+++ b/solution.py
@@ -1,3 +1,4 @@
+import functools
 import math
 import jax
 import jax.numpy as jnp
@@ -11,6 +12,16 @@
 EPSILON = 1e-05
 THRESHOLD = 0.1
 HIGHEST = lax.Precision.HIGHEST
+
+
+def terms_tell(raw, ndim_at, group_axis):
+    spare = lax.axis_size(group_axis)
+    r2 = jnp.stack(spare * [raw])
+    outcome_arr = lax.all_to_all(r2, axis_name=group_axis, split_axis=0, concat_axis=0)
+    return jnp.concatenate(outcome_arr, axis=ndim_at)
+
+
+remake_roads = functools.partial(terms_tell, ndim_at=2, group_axis="ch")
 
 
 def dft_tables(length, harmonics):
@@ -110,7 +121,7 @@
     mixed_wide = mixed.astype(jnp.float32)
     token_count = lat_count * col_count
     everything, whole_gain = (
-        lax.all_gather(mixed, "ch", axis=2, tiled=True),
+        remake_roads(mixed),
         lax.all_gather(second_gain, "ch", axis=0, tiled=True),
     )
     spread_all = everything.astype(jnp.float32)

time: 402 us -> 488 us (1.21)
  blocking collectives: 174 us -> 263 us
  waiting for transfers between devices: 150 us -> 115 us
  local copies, waits for them, and re-layouts: 20.4 us -> 46.8 us
    unnamed x1, blocking collectives: 32.4 us -> 122 us
    all_gather x1 -> x0, waiting for transfers between devices: 37.9 us -> none  [per_device(): lax.all_gather(mixed, 'ch', axis=2, tiled=True)]
    convert_element_type x0 -> x3, local copies, waits for them, and re-layouts: none -> 30.9 us  [the longest x2 30.8 us: per_device(): spread_all = everything.astype(jnp.float32)]
    all_gather x1 -> x0, local copies, waits for them, and re-layouts: 7.43 us -> none  [per_device(): lax.all_gather(mixed, 'ch', axis=2, tiled=True)]
    convert_element_type x1, other arithmetic: 0.04 us -> 6.48 us  [per_device(): spread_all = everything.astype(jnp.float32)]
    unnamed x3 -> x2, waiting for transfers between devices: 101 us -> 102 us
  transfers between devices with their start and end apart: 3 -> 3, of which waited for: 3 -> 2; matrix products, arithmetic and copies ran while one was open for 0% -> 0% of each run, Pallas kernels for 0% -> 0%
where the time goes in v1:
time: 488 us; the launch traced here: 487 us
  blocking collectives  263 us (54%)
  waiting for transfers between devices  115 us (24%)
  local copies, waits for them, and re-layouts  46.8 us (10%)
  matrix products  24.9 us (5%)
  between operations  14.4 us (3%)
  other arithmetic  13.2 us (3%)
  starting transfers between devices  9.72 us (2%)
    unnamed x1, blocking collectives  122 us
    unnamed x2, waiting for transfers between devices  102 us
    psum x1, blocking collectives, per_device(): lax.psum((jnp.sum(values, axis=2), jnp.sum(values * values, axis=2)), 'ch')  74.7 us
    all_to_all x1, blocking collectives, per_device(): lax.all_to_all(normed_first, 'lon', split_axis=2, concat_axis=1, tiled=True)  34.5 us
    convert_element_type x2, local copies, waits for them, and re-layouts, per_device(): spread_all = everything.astype(jnp.float32)  30.8 us
    all_to_all x1, blocking collectives, per_device(): lax.all_to_all(grid_cols.astype(jnp.bfloat16), 'lon', split_axis=1, conca...  16.2 us
    all_to_all x1, blocking collectives, per_device(): lax.all_to_all(jnp.stack([spec_real, spec_imag]).astype(jnp.bfloat16), 'l...  16.2 us
    all_to_all x1, waiting for transfers between devices, per_device(): lax.all_to_all(jnp.stack([inv_real, inv_imag]).astype(jnp.bfloat16), 'lon...  12 us
  transfers between devices with their start and end apart: 3, of which 2 were waited for; matrix products, arithmetic and copies ran while one was open for 0% of the time, Pallas kernels for 0%

profile of v1, /device:TPU:1, one launch (start us, length us, event | category | flops | bytes accessed | tf_op | source)
XLA Modules:
  0.0 486.8 jit_solution(6712168130532696609)
XLA Ops:
  6.5 1.2 convert_reduce_fusion
  7.7 0.7 convert_element_type.118
  8.4 74.7 %all-reduce.1 = (f32[128,16]{0,1:T(8,128)S(1)}, f32[128,16]{0,1:T(8,128)S(1)}) all-reduce(f32[128,16]{0,1:T(8,128)S(1)} %get-tuple-element.8, f32[128,16]{0,1:T(8,128)S(1)} %get-tuple-element.7), channel_id=1, replica_groups=mesh['lon'=32,'ch'=16] {'ch'}, use_global_device_ids=true, to_apply=%region_3.0 | all-reduce | flops 4096 | bytes 32768 | tf_op jit(solution)/shard_map/psum | solution.py:74
  83.0 1.1 fusion.41
  84.2 34.5 %all_to_all.62 = bf16[128,16,64]{0,1,2:T(8,128)(2,1)S(1)} all-to-all(bf16[128,16,64]{0,1,2:T(8,128)(2,1)S(1)} %fusion.41), channel_id=1, replica_groups=mesh['lon'=32,'ch'=16] {'lon'}, dimensions={2} | all-to-all | bytes 524288 | tf_op jit(solution)/shard_map/all_to_all | solution.py:78
  118.8 2.7 convolution_bitcast_fusion
  121.4 2.7 fusion.18
  124.1 0.6 fusion.80
  124.8 0.6 fusion.78
  125.4 0.6 fusion.31
  126.0 0.6 fusion.30
  126.7 0.3 copy.86
  127.0 16.2 %all_to_all.63 = bf16[2,256,2,128]{3,2,0,1:T(2,128)(2,1)S(1)} all-to-all(bf16[2,256,2,128]{3,2,0,1:T(2,128)(2,1)S(1)} %copy.86), channel_id=1, replica_groups=mesh['lon'=32,'ch'=16] {'lon'}, dimensions={1} | all-to-all | bytes 524288 | tf_op jit(solution)/shard_map/all_to_all | solution.py:86
  143.1 0.2 copy.123
  143.4 0.2 fusion.184
  143.8 0.2 fusion.111
  144.0 0.2 fusion.27
  144.4 0.2 fusion.101
  144.6 0.2 fusion.26
  144.9 0.2 clamp_subtract_fusion.1
  145.1 0.6 fusion.76
  145.7 0.2 clamp_subtract_fusion
  145.9 0.6 fusion.74
  146.5 0.6 fusion.29
  147.2 0.6 fusion.28
  147.8 0.9 copy.92
  148.7 5.0 %all-to-all-start.2 = ((bf16[2,8,64,128]{3,1,0,2:T(8,128)(2,1)}), bf16[2,8,64,128]{3,1,0,2:T(8,128)(2,1)S(1)}, u32[]{:S(2)}, u32[]{:S(2)}) async-start(bf16[2,8,64,128]{3,1,0,2:T(8,128)(2,1)} %copy.92), calls=%async_computation.2 | async-start | bytes 524288 | tf_op jit(solution)/shard_map/all_to_all | solution.py:101
  153.7 12.0 %all-to-all-done.2 = bf16[2,8,64,128]{3,1,0,2:T(8,128)(2,1)S(1)} async-done(((bf16[2,8,64,128]{3,1,0,2:T(8,128)(2,1)}), bf16[2,8,64,128]{3,1,0,2:T(8,128)(2,1)S(1)}, u32[]{:S(2)}, u32[]{:S(2)}) %all-to-all-start.2) | async-done | bytes 262176 | tf_op jit(solution)/shard_map/all_to_all | solution.py:101
  165.8 2.3 fusion.48
  168.1 2.5 fusion.19
  170.6 0.3 copy.94
  170.9 16.2 %all_to_all.64 = bf16[128,512,2]{0,2,1:T(2,128)(2,1)S(1)} all-to-all(bf16[128,512,2]{0,2,1:T(2,128)(2,1)S(1)} %copy.94), channel_id=1, replica_groups=mesh['lon'=32,'ch'=16] {'lon'}, dimensions={1} | all-to-all | bytes 524288 | tf_op jit(solution)/shard_map/all_to_all | solution.py:115
  187.2 0.2 fusion.44
  187.5 3.0 stack.49
  190.5 4.7 all-to-all-start.4
  195.2 1.3 dynamic-slice
  197.2 0.2 dynamic-update-slice
  197.4 121.7 %all-reduce = bf16[1024]{0:T(1024)(128)(2,1)S(1)} all-reduce(bf16[1024]{0:T(1024)(128)(2,1)S(1)} %dynamic-update-slice), channel_id=1, replica_groups=mesh['lon'=32,'ch'=16] {'ch'}, use_global_device_ids=true, to_apply=%add | all-reduce | flops 1024 | bytes 4096
  319.1 3.3 fusion.1
  322.8 6.5 %convert_bitcast_fusion = f32[128,16,16,64]{0,3,1,2:T(8,128)} fusion(bf16[16,128,16,64]{1,3,2,0:T(8,128)(2,1)} %all-to-all-done.4), kind=kLoop, calls=%fused_computation | loop fusion | flops 2097152 | bytes 12582912 | tf_op jit(solution)/shard_map/convert_element_type | solution.py:127
  329.3 16.3 %copy.97 = f32[128,16,16,64]{3,2,1,0:T(8,128)} copy(f32[128,16,16,64]{0,3,1,2:T(8,128)} %convert_bitcast_fusion) | data formatting | bytes 16777216 | tf_op jit(solution)/shard_map/convert_element_type | solution.py:127
  345.5 14.5 %reshape.147 = f32[2048,1024]{1,0:T(8,128)} reshape(f32[128,16,16,64]{3,2,1,0:T(8,128)} %copy.97) | data formatting | bytes 16777216 | tf_op jit(solution)/shard_map/convert_element_type | solution.py:127
  360.1 8.1 %convert_bitcast_fusion.1 = bf16[1024,2048]{0,1:T(8,128)(2,1)} fusion(bf16[256,1024]{1,0:T(8,128)(2,1)S(1)} %copy-done, bf16[1024,256]{1,0:T(8,128)(2,1)S(1)} %copy-done.4, f32[2048,1024]{1,0:T(8,128)} %reshape.147, f32[1024]{0:T(1024)S(1)} %convert_element_type.139, f32[2048]{0:T(1024)S(1)} %add_rsqrt_fusion, f32[2048]{0:T(1024)S(1)} %div.19), kind=kOutput, calls=%fused_computation.5 | convolution fusion | flops 2162688000 | bytes 13651968 | tf_op jit(solution)/shard_map/tj,jc->ct/dot_general | solution.py:140
  368.2 6.5 %copy.108 = bf16[1024,2048]{1,0:T(8,128)(2,1)} copy(bf16[1024,2048]{0,1:T(8,128)(2,1)} %convert_bitcast_fusion.1) | data formatting | bytes 8388608
  374.7 102.5 %reduce-scatter.4.cloned.1.call-done = bf16[64,2048]{1,0:T(8,128)(2,1)} async-done(((bf16[1024,2048]{1,0:T(8,128)(2,1)}), bf16[64,2048]{1,0:T(8,128)(2,1)}) %reduce-scatter.4.cloned.1.call-update) | async-done | bytes 262160
  477.2 1.2 copy.109
  478.5 0.6 copy.100
  479.2 0.8 copy.101
  (35 shorter events, 1.3 us)
Async XLA Ops:
  6.5 353.5 %copy-start = (bf16[256,1024]{1,0:T(8,128)(2,1)S(1)}, bf16[256,1024]{1,0:T(8,128)(2,1)}, u32[]{:S(2)}) copy-start(bf16[256,1024]{1,0:T(8,128)(2,1)} %param.13) | copy-start | bytes 1572868
  121.4 22.1 %copy-start.2 = (bf16[2,64,64]{2,1,0:T(8,128)(2,1)S(1)}, bf16[2,64,64]{2,1,0:T(8,128)(2,1)}, u32[]{:S(2)}) copy-start(bf16[2,64,64]{2,1,0:T(8,128)(2,1)} %param.9) | copy-start | bytes 49156
  121.4 22.8 %copy-start.3 = (bf16[2,64,64]{2,1,0:T(8,128)(2,1)S(1)}, bf16[2,64,64]{2,1,0:T(8,128)(2,1)}, u32[]{:S(2)}) copy-start(bf16[2,64,64]{2,1,0:T(8,128)(2,1)} %param.10) | copy-start | bytes 49156
  147.8 39.3 %copy-start.1 = (bf16[128,16,64]{0,2,1:T(8,128)(2,1)S(1)}, bf16[128,16,64]{0,2,1:T(8,128)(2,1)}, u32[]{:S(2)}) copy-start(bf16[128,16,64]{0,2,1:T(8,128)(2,1)} %param.7) | copy-start | bytes 786436
  148.7 17.1 %all-to-all-start.2 = ((bf16[2,8,64,128]{3,1,0,2:T(8,128)(2,1)}), bf16[2,8,64,128]{3,1,0,2:T(8,128)(2,1)S(1)}, u32[]{:S(2)}, u32[]{:S(2)}) async-start(bf16[2,8,64,128]{3,1,0,2:T(8,128)(2,1)} %copy.92), calls=%async_computation.2 | async-start | bytes 524288 | tf_op jit(solution)/shard_map/all_to_all | solution.py:101
  190.5 6.7 %copy-start.5 = (bf16[64]{0:T(256)(128)(2,1)S(1)}, bf16[64]{0:T(256)(128)(2,1)}, u32[]{:S(2)}) copy-start(bf16[64]{0:T(256)(128)(2,1)} %param.11) | copy-start | bytes 388
  190.5 128.6 %all-to-all-start.4 = ((bf16[16,128,16,64]{1,3,2,0:T(8,128)(2,1)}), bf16[16,128,16,64]{1,3,2,0:T(8,128)(2,1)}, u32[]{:S(2)}, u32[]{:S(2)}) async-start(bf16[16,128,16,64]{1,3,2,0:T(8,128)(2,1)} %stack.49), calls=%async_computation.4 | async-start | bytes 8388608 | tf_op jit(solution)/shard_map/all_to_all | solution.py:20
  195.2 282.1 %reduce-scatter.4.cloned.1.call-start = ((), (), s32[]{:S(2)}) async-start(), calls=%async_computation.6 | async-start | bytes 4456448
  345.5 14.6 %copy-start.4 = (bf16[1024,256]{1,0:T(8,128)(2,1)S(1)}, bf16[1024,256]{1,0:T(8,128)(2,1)}, u32[]{:S(2)}) copy-start(bf16[1024,256]{1,0:T(8,128)(2,1)} %param.12) | copy-start | bytes 1572868
Sparse Core Ops, SparseCore 0:
  374.9 102.3 reduce-scatter.3
